TPU v7x, 1024 devices: a whole 8x8x8 slice. The times are simulated.
1024 devices in a mesh: group: 64 (over x, y), local: 16 (over z, core).
Axes of the slice: x: 8, y: 8, z: 8, core: 2. Of those that a mesh axis runs over, the one named last changes fastest.
Arguments:
- out_grad: bfloat16 [8192, 7168], P('group', 'local'), may hold values from -6 to 6
- route_groups: int32 [8192, 4], P('group'), may hold values from 0 to 63, as said below
- route_slots: int32 [8192, 4], P('group'), may hold values from 0 to 15, as said below
- route_drops: int32 [8192, 4], P('group'), may hold values 0 or 1
- combine: bfloat16 [8192, 4], P('group'), may hold values from 0.099609375 to 1
- gate_pre: bfloat16 [64, 1024, 1024], P('group'), may hold values from -8 to 8
- up_pre: bfloat16 [64, 1024, 1024], P('group'), may hold values from -6 to 6
- w_gate: bfloat16 [64, 7168, 1024], P('group', 'local'), may hold values from -0.0625 to 0.0625
- w_up: bfloat16 [64, 7168, 1024], P('group', 'local'), may hold values from -0.0625 to 0.0625
- w_down: bfloat16 [64, 1024, 7168], P('group', None, 'local'), may hold values from -0.1875 to 0.1875
Outputs:
- in_grad: bfloat16 [8192, 7168], P('group', 'local')
Inputs may be any that keep to these rules, and one draw needn't show every extreme that they name: `route_groups`: each token names 4 different groups. Among the tokens of one source group (aligned blocks of 128 tokens) no group is named more than 16 times, and some group exactly 16 times in every block. `route_slots`: within one source group's tokens, the routes to one group have different slots; dropped routes have slots too.
All inputs are finite; a program needn't handle non-finite values. No bound on the sum of `route_drops` on one device may be relied on, other than what follows from the above.
Results may differ from a plain program's by a relative error of at most 0.027.
Values may be sent and summed in bfloat16 or wider, within the bound.
A program may use at most 64 MiB of HBM per device.

v0:
```python
import jax
import jax.numpy as jnp
from jax import lax
from jax.sharding import PartitionSpec as P


def swiglu_grad(raw_sums, gate_vals, up_vals, slot_weight):
    gate_f = gate_vals.astype(jnp.float32)
    up_f = up_vals.astype(jnp.float32)
    sigmoid_gate = jax.nn.sigmoid(gate_f)
    hidden_grad = raw_sums * slot_weight[None, :]
    gate_grad = (hidden_grad * up_f * sigmoid_gate * (1.0 + gate_f * (1.0 - sigmoid_gate))).astype(
        jnp.bfloat16
    )
    up_grad = (hidden_grad * gate_f * sigmoid_gate).astype(jnp.bfloat16)
    return (gate_grad, up_grad)


def shards(
    out_grad,
    route_groups,
    route_slots,
    route_drops,
    combine,
    gate_pre,
    up_pre,
    w_gate,
    w_up,
    w_down,
):
    groups_count = lax.axis_size("group")
    feature_cols = out_grad.shape[1]
    capacity = gate_pre.shape[2] // groups_count
    target = route_groups * capacity + route_slots
    places = lax.iota(jnp.int32, groups_count * capacity)
    matches = (places[:, None, None] == target[None]) & (route_drops[None] == 0)
    onehot = jnp.any(matches, axis=2).astype(jnp.bfloat16)
    weight_col = jnp.sum(
        jnp.where(matches, combine.astype(jnp.float32)[None], 0.0), axis=(1, 2)
    ).astype(jnp.bfloat16)
    send_rows = jnp.dot(onehot, out_grad, preferred_element_type=jnp.float32).astype(jnp.bfloat16)
    received, got_weight = (
        lax.all_to_all(
            send_rows.reshape(groups_count, capacity, feature_cols),
            "group",
            split_axis=0,
            concat_axis=0,
            tiled=True,
        ),
        lax.all_to_all(
            weight_col.reshape(groups_count, capacity),
            "group",
            split_axis=0,
            concat_axis=0,
            tiled=True,
        ),
    )
    slot_rows = received.reshape(-1, feature_cols)
    slot_weight = got_weight.reshape(-1).astype(jnp.float32)
    gate_all = gate_pre[0]
    up_all = up_pre[0]
    gate_weights = w_gate[0]
    up_weights = w_up[0]
    down_weights = w_down[0]
    partial_sums = jnp.einsum(
        "hd,sd->hs", down_weights, slot_rows, preferred_element_type=jnp.float32
    )
    raw_sums = lax.psum(partial_sums.astype(jnp.bfloat16), "local").astype(jnp.float32)
    gate_grad, up_grad = swiglu_grad(raw_sums, gate_all, up_all, slot_weight)
    totals = jnp.einsum("hs,dh->sd", gate_grad, gate_weights, preferred_element_type=jnp.float32)
    totals = totals + jnp.einsum(
        "hs,dh->sd", up_grad, up_weights, preferred_element_type=jnp.float32
    )
    slot_grad = totals.astype(jnp.bfloat16)
    returned = lax.all_to_all(
        slot_grad.reshape(groups_count, capacity, feature_cols),
        "group",
        split_axis=0,
        concat_axis=0,
        tiled=True,
    )
    returned_rows = returned.reshape(-1, feature_cols)
    token_grad = lax.dot_general(
        onehot, returned_rows, (((0,), (0,)), ((), ())), preferred_element_type=jnp.float32
    )
    return token_grad.astype(jnp.bfloat16)


def solution(mesh):
    placed = (
        P("group", "local"),
        P("group", None),
        P("group", None),
        P("group", None),
        P("group", None),
        P("group", None, None),
        P("group", None, None),
        P("group", "local", None),
        P("group", "local", None),
        P("group", None, "local"),
    )
    return jax.shard_map(
        shards, mesh=mesh, in_specs=placed, out_specs=P("group", "local"), check_vma=False
    )
```

profile of v0, /device:TPU:1, one launch (start us, length us, event | category | flops | bytes accessed | tf_op | source)
XLA Modules:
  0.0 245.0 jit_solution(8104326220157962346)
XLA Ops:
  6.5 0.0 copy-start
  6.5 0.0 all-reduce.2.cloned.1.call-start
  6.5 0.8 broadcast_compare_fusion
  7.3 0.7 multiply_add_fusion
  8.0 0.3 fusion.10
  8.3 1.3 convolution_convert_fusion
  9.6 0.5 copy.31
  10.2 37.0 %all_to_all.16 = bf16[64,16,448]{2,1,0:T(8,128)(2,1)S(1)} all-to-all(bf16[64,16,448]{2,1,0:T(8,128)(2,1)S(1)} %bitcast.33), channel_id=1, replica_groups=mesh['group'=64,'local'=16] {'group'}, dimensions={0} | all-to-all | bytes 1835008 | tf_op jit(solution)/shard_map/all_to_all | solution.py:43
  47.2 0.0 copy-done
  47.2 2.6 %convert_bitcast_fusion = bf16[1024,1024]{0,1:T(8,128)(2,1)} fusion(bf16[1024,448]{1,0:T(8,128)(2,1)S(1)} %bitcast.35, bf16[1,1024,448]{1,2,0:T(8,128)(2,1)S(1)} %copy-done), kind=kOutput, calls=%fused_computation.15 | convolution fusion | flops 940572672 | bytes 3932160 | tf_op jit(solution)/shard_map/hd,sd->hs/dot_general | solution.py:65
  49.7 0.0 copy-start.3
  49.7 0.0 copy-start.1
  49.8 0.0 all-reduce.2.cloned.1.call-update
  49.8 0.7 copy-done.3
  50.4 0.5 select_reduce_fusion
  50.9 0.7 convert_element_type.84
  51.6 11.3 %all-to-all-start.1 = ((bf16[64,1,16]{2,1,0:T(2,128)(2,1)}), bf16[64,1,16]{2,1,0:T(2,128)(2,1)S(1)}, u32[]{:S(2)}, u32[]{:S(2)}) async-start(bf16[64,1,16]{2,1,0:T(2,128)(2,1)} %convert_element_type.84), calls=%async_computation.1 | async-start | bytes 65536 | tf_op jit(solution)/shard_map/all_to_all | solution.py:50
  63.0 0.0 copy-done.1
  63.0 2.6 %copy.34 = bf16[1,1024,1024]{1,2,0:T(8,128)(2,1)} copy(bf16[1,1024,1024]{2,1,0:T(8,128)(2,1)S(1)} %copy-done.1) | data formatting | bytes 4194304 | tf_op args[5]
  65.6 0.0 copy-start.2
  65.6 4.1 %copy.33 = bf16[1,1024,1024]{1,2,0:T(8,128)(2,1)} copy(bf16[1,1024,1024]{2,1,0:T(8,128)(2,1)} %param.16) | data formatting | bytes 4194304 | tf_op args[6]
  69.7 4.1 %all-to-all-done.1 = bf16[64,1,16]{2,1,0:T(2,128)(2,1)S(1)} async-done(((bf16[64,1,16]{2,1,0:T(2,128)(2,1)}), bf16[64,1,16]{2,1,0:T(2,128)(2,1)S(1)}, u32[]{:S(2)}, u32[]{:S(2)}) %all-to-all-start.1) | async-done | bytes 2080 | tf_op jit(solution)/shard_map/all_to_all | solution.py:50
  73.7 0.1 convert_reduce_fusion
  73.8 0.1 reshape.48
  73.9 115.2 %all-reduce.2.cloned.1.call-done = bf16[1024,1024]{0,1:T(8,128)(2,1)} async-done(((bf16[1024,1024]{0,1:T(8,128)(2,1)}), bf16[1024,1024]{0,1:T(8,128)(2,1)}) %all-reduce.2.cloned.1.call-update) | async-done | bytes 2097168 | tf_op jit(solution)/shard_map/psum | solution.py:68
  189.0 0.0 copy-done.2
  189.0 0.0 copy-start.4
  189.1 0.0 copy-start.5
  189.1 5.1 %fusion.13 = f32[1024,448]{0,1:T(8,128)S(1)} fusion(bf16[1024,1024]{0,1:T(8,128)(2,1)} %all-reduce.2.cloned.1.call-done, bf16[1,1024,1024]{1,2,0:T(8,128)(2,1)} %copy.33, bf16[1,1024,1024]{1,2,0:T(8,128)(2,1)S(1)} %copy-done.2, f32[1024]{0:T(1024)S(1)} %reshape.48, bf16[1,448,1024]{2,1,0:T(8,128)(2,1)} %param.17), kind=kOutput, calls=%fused_computation.20 | convolution fusion | flops 954204160 | bytes 9048064 | tf_op jit(solution)/shard_map/hs,dh->sd/dot_general | solution.py:70
  194.2 0.0 copy-done.4
  194.2 0.0 copy-done.5
  194.2 2.8 %add_convert_fusion = bf16[1024,448]{0,1:T(8,128)(2,1)} fusion(f32[1024,448]{0,1:T(8,128)S(1)} %fusion.13, bf16[1024,1024]{0,1:T(8,128)(2,1)S(1)} %copy-done.4, bf16[1,1024,1024]{1,2,0:T(8,128)(2,1)S(1)} %copy-done.2, f32[1024]{0:T(1024)S(1)} %reshape.48, bf16[1,448,1024]{2,1,0:T(8,128)(2,1)S(1)} %copy-done.5), kind=kOutput, calls=%fused_computation.21 | convolution fusion | flops 949878784 | bytes 7868416 | tf_op jit(solution)/shard_map/hs,dh->sd/dot_general | solution.py:71
  197.0 1.5 copy.35
  198.5 38.5 %all_to_all.17 = bf16[64,16,448]{2,1,0:T(8,128)(2,1)S(1)} all-to-all(bf16[64,16,448]{2,1,0:T(8,128)(2,1)S(1)} %bitcast.34), channel_id=1, replica_groups=mesh['group'=64,'local'=16] {'group'}, dimensions={0} | all-to-all | bytes 1835008 | tf_op jit(solution)/shard_map/all_to_all | solution.py:75
  237.0 1.2 convolution_convert_fusion.1
  (1 shorter events, 0.0 us)
Async XLA Ops:
  6.5 40.6 %copy-start = (bf16[1,1024,448]{1,2,0:T(8,128)(2,1)S(1)}, bf16[1,1024,448]{1,2,0:T(8,128)(2,1)}, u32[]{:S(2)}) copy-start(bf16[1,1024,448]{1,2,0:T(8,128)(2,1)} %param.19) | copy-start | bytes 2752516
  6.5 182.5 %all-reduce.2.cloned.1.call-start = ((), (), s32[]{:S(2)}) async-start(), calls=%async_computation.3 | async-start | bytes 4194304 | tf_op jit(solution)/shard_map/psum | solution.py:68
  49.7 0.7 copy-start.3
  49.7 13.2 %copy-start.1 = (bf16[1,1024,1024]{2,1,0:T(8,128)(2,1)S(1)}, bf16[1,1024,1024]{2,1,0:T(8,128)(2,1)}, u32[]{:S(2)}) copy-start(bf16[1,1024,1024]{2,1,0:T(8,128)(2,1)} %param.15) | copy-start | bytes 6291460
  51.6 22.1 %all-to-all-start.1 = ((bf16[64,1,16]{2,1,0:T(2,128)(2,1)}), bf16[64,1,16]{2,1,0:T(2,128)(2,1)S(1)}, u32[]{:S(2)}, u32[]{:S(2)}) async-start(bf16[64,1,16]{2,1,0:T(2,128)(2,1)} %convert_element_type.84), calls=%async_computation.1 | async-start | bytes 65536 | tf_op jit(solution)/shard_map/all_to_all | solution.py:50
  65.6 123.5 %copy-start.2 = (bf16[1,1024,1024]{1,2,0:T(8,128)(2,1)S(1)}, bf16[1,1024,1024]{1,2,0:T(8,128)(2,1)}, u32[]{:S(2)}) copy-start(bf16[1,1024,1024]{1,2,0:T(8,128)(2,1)} %copy.34) | copy-start | bytes 6291460
  189.0 5.1 %copy-start.4 = (bf16[1024,1024]{0,1:T(8,128)(2,1)S(1)}, bf16[1024,1024]{0,1:T(8,128)(2,1)}, u32[]{:S(2)}) copy-start(bf16[1024,1024]{0,1:T(8,128)(2,1)} %all-reduce.2.cloned.1.call-done) | copy-start | bytes 6291460
  189.1 5.1 %copy-start.5 = (bf16[1,448,1024]{2,1,0:T(8,128)(2,1)S(1)}, bf16[1,448,1024]{2,1,0:T(8,128)(2,1)}, u32[]{:S(2)}) copy-start(bf16[1,448,1024]{2,1,0:T(8,128)(2,1)} %param.18) | copy-start | bytes 2752516
Sparse Core Ops, SparseCore 0:
  49.9 139.1 all-reduce.1
where the time goes:
time: 249 us; the launch traced here: 245 us
  waiting for transfers between devices  119 us (48%)
  blocking collectives  75.5 us (30%)
  between operations  13.5 us (5%)
  matrix products  13 us (5%)
  starting transfers between devices  11.3 us (5%)
  local copies, waits for them, and re-layouts  10.1 us (4%)
    psum x1, waiting for transfers between devices, shards(): lax.psum(partial_sums.astype(jnp.bfloat16), 'local').astype(jnp.float32)  115 us
    all_to_all x1, blocking collectives, shards(): lax.all_to_all(slot_grad.reshape(groups_count, capacity, feature_cols), '...  38.5 us
    all_to_all x1, blocking collectives, shards(): lax.all_to_all(send_rows.reshape(groups_count, capacity, feature_cols), '...  37 us
    all_to_all x1, starting transfers between devices, shards(): lax.all_to_all(weight_col.reshape(groups_count, capacity), 'group', split...  11.3 us
    unnamed x14, local copies, waits for them, and re-layouts  7.36 us
    dot_general x1, matrix products, shards(): jnp.einsum('hs,dh->sd', gate_grad, gate_weights, preferred_element_type=j...  5.11 us
  transfers between devices with their start and end apart: 2, of which 2 were waited for; matrix products, arithmetic and copies ran while one was open for 3% of the time, Pallas kernels for 0%

commit v1 on v0

v1 whole, which is shorter than its diff:
```python
import functools
import math

import jax
import jax.numpy as jnp
from jax import lax
from jax.experimental import pallas as pl
from jax.experimental.pallas import tpu as pltpu
from jax.sharding import PartitionSpec as P

MESH = pl.DeviceIdType.MESH
F32 = jnp.float32
BF16 = jnp.bfloat16
HEAD = 16


def streams(n):
    long, short = n // 2, max(n // 2 - 1, 0)
    return ((1, 0, long), (-1, 1, long), (1, 1, short), (-1, 0, short))


def ring_gather(pos, n, device, view, send_sem, recv_sem, landed=None):
    def copy(stream, step, owner):
        sign, half, _ = streams(n)[stream]
        place = view(owner, half)
        return pltpu.make_async_remote_copy(
            src_ref=place,
            dst_ref=place,
            send_sem=send_sem.at[stream, step],
            recv_sem=recv_sem.at[stream, step],
            device_id=device(lax.rem(pos + sign + n, n)),
            device_id_type=MESH,
        )

    def owner_of(sign, step):
        return lax.rem(pos - sign * step + n, n)

    sent = []
    for step in range(n // 2 + 1):
        for stream, (sign, half, steps) in enumerate(streams(n)):
            if 0 < step <= steps:
                owner = owner_of(sign, step)
                copy(stream, step - 1, owner).wait_recv()
            if step < steps:
                going = copy(stream, step, owner_of(sign, step))
                going.start()
                sent.append(going)
            if 0 < step <= steps and landed is not None:
                landed(stream, step - 1, owner, half)
    return sent


def ring_sum(pos, n, device, term, out_buf, in_buf, send_sem, recv_sem):
    def copy(stream, step):
        sign = streams(n)[stream][0]
        return pltpu.make_async_remote_copy(
            src_ref=out_buf.at[stream, step],
            dst_ref=in_buf.at[stream, step],
            send_sem=send_sem.at[stream, step],
            recv_sem=recv_sem.at[stream, step],
            device_id=device(lax.rem(pos + sign + n, n)),
            device_id_type=MESH,
        )

    sent = []
    for step in range(n // 2):
        for stream, (sign, half, steps) in enumerate(streams(n)):
            if step >= steps:
                continue
            value = term(lax.rem(pos + sign * (steps - step) + n, n), half)
            if step > 0:
                copy(stream, step - 1).wait_recv()
                value = value + in_buf[stream, step - 1].astype(F32)
            out_buf[stream, step] = value.astype(BF16)
            going = copy(stream, step)
            going.start()
            sent.append(going)
    sums = []
    for half in range(2):
        value = term(pos, half)
        for stream, (sign, which, steps) in enumerate(streams(n)):
            if which == half and steps > 0:
                copy(stream, steps - 1).wait_recv()
                value = value + in_buf[stream, steps - 1].astype(F32)
        sums.append(value)
    return sums, sent


def kernel(
    side,
    depth,
    cap,
    ext_ref,
    gate_hbm,
    up_hbm,
    wg_hbm,
    wu_hbm,
    wd_hbm,
    out_ref,
    gate_v,
    up_v,
    wg_v,
    wu_v,
    wd_v,
    gate_f,
    up_f,
    toks,
    picks,
    order,
    msg_out,
    msg_in,
    rows,
    sib_out,
    sib_in,
    acc,
    zs_out,
    zs_in,
    raw,
    grad,
    ret_out,
    ret_in,
    part,
    fs_out,
    fs_in,
    load_sem,
    tg_send,
    tg_recv,
    a2a_send,
    a2a_recv,
    sib_send,
    sib_recv,
    zs_send,
    zs_recv,
    zg_send,
    zg_recv,
    sg_send,
    sg_recv,
    ret_send,
    ret_recv,
    fs_send,
    fs_recv,
):
    group, local = lax.axis_index("group"), lax.axis_index("local")
    core, z = lax.rem(local, 2), lax.div(local, 2)
    gx, gy = lax.div(group, side), lax.rem(group, side)
    first = gx + core * (gy - gx)
    second = gy + core * (gx - gy)
    first_step = side - core * (side - 1)
    second_step = 1 + core * (side - 1)
    sibling = (group, local + 1 - 2 * core)
    tokens = ext_ref.shape[1]
    feats = out_ref.shape[0]
    slots = gate_v.shape[1]
    hidden = gate_v.shape[0]
    block = side * cap
    half_hid = hidden // 2
    chunk = half_hid // depth
    half_slots = slots // 2

    def at_first(f):
        return (f * first_step + second * second_step, local)

    def at_second(s):
        return (first * first_step + s * second_step, local)

    def at_z(q):
        return (group, q * 2 + core)

    loads = [
        pltpu.make_async_copy(src, dst, load_sem.at[i])
        for i, (src, dst) in enumerate(
            ((gate_hbm, gate_v), (up_hbm, up_v), (wd_hbm, wd_v), (wg_hbm, wg_v), (wu_hbm, wu_v))
        )
    ]
    for load in loads:
        load.start()

    barrier = pltpu.get_barrier_semaphore()
    peers = [at_first(lax.rem(first + 1, side)), at_first(lax.rem(first + side - 1, side))]
    peers += [at_second(lax.rem(second + d, side)) for d in range(1, side)]
    if depth > 1:
        peers += [at_z(lax.rem(z + 1, depth)), at_z(lax.rem(z + depth - 1, depth))]
    peers += [sibling]
    for peer in peers:
        pl.semaphore_signal(barrier, inc=1, device_id=peer, device_id_type=MESH)
    toks[:, pl.ds(pl.multiple_of(first * tokens, tokens), tokens)] = ext_ref[...]
    picks[...] = jnp.zeros_like(picks)
    pl.semaphore_wait(barrier, len(peers))

    tok_rows = toks.shape[0]
    cut = (tok_rows // 32) * 16

    def tok_view(owner, half):
        span = pl.ds(0, cut) if half == 0 else pl.ds(cut, tok_rows - cut)
        return toks.at[span, pl.ds(pl.multiple_of(owner * tokens, tokens), tokens)]

    sent = ring_gather(first, side, at_first, tok_view, tg_send, tg_recv)

    @pl.loop(0, side)
    def _(f):
        lanes = pl.ds(pl.multiple_of(f * tokens, tokens), tokens)
        table = toks[pl.ds(feats, HEAD), lanes].astype(F32)
        place = table[4:8] * cap + table[8:12]
        slot = lax.broadcasted_iota(jnp.int32, (cap, tokens), 0)
        for e in range(side):
            wanted = ((first * first_step + e * second_step) * cap + slot).astype(F32)
            hit = wanted == place[0:1]
            for j in range(1, 4):
                hit = hit | (wanted == place[j : j + 1])
            at = pl.ds(pl.multiple_of(e * block + f * cap, cap), cap)
            picks[at, lanes] = jnp.where(hit, 1.0, 0.0).astype(BF16)

    def exchange_copy(d, out_buf, in_buf, send_sem, recv_sem):
        return pltpu.make_async_remote_copy(
            src_ref=out_buf.at[:, pl.ds(pl.multiple_of(d * block, block), block)],
            dst_ref=in_buf.at[:, pl.ds(pl.multiple_of(second * block, block), block)],
            send_sem=send_sem.at[d],
            recv_sem=recv_sem.at[d],
            device_id=at_second(lax.rem(second + d, side)),
            device_id_type=MESH,
        )

    def exchange_start(left, matrix, out_buf, in_buf, send_sem, recv_sem):
        @pl.loop(0, side)
        def _(i):
            d = lax.rem(i + side // 2, side)
            e = lax.rem(second + d, side)
            picked = matrix[pl.ds(pl.multiple_of(e * block, block), block), :]
            message = lax.dot_general(
                left[...], picked, (((1,), (1,)), ((), ())), preferred_element_type=F32
            ).astype(BF16)

            @pl.when(d == 0)
            def _():
                in_buf[:, pl.ds(pl.multiple_of(second * block, block), block)] = message

            @pl.when(d != 0)
            def _():
                out_buf[:, pl.ds(pl.multiple_of(d * block, block), block)] = message
                exchange_copy(d, out_buf, in_buf, send_sem, recv_sem).start()

    def exchange_wait(out_buf, in_buf, send_sem, recv_sem):
        @pl.loop(1, side)
        def _(d):
            exchange_copy(d, out_buf, in_buf, send_sem, recv_sem).wait()

    exchange_start(toks, picks, msg_out, msg_in, a2a_send, a2a_recv)

    loads[0].wait()
    loads[1].wait()
    strip = 16

    @pl.loop(0, hidden // strip)
    def _(i):
        at = pl.ds(pl.multiple_of(i * strip, strip), strip)
        a = gate_v[at, :].astype(F32)
        b = up_v[at, :].astype(F32)
        s = jax.nn.sigmoid(a)
        gate_f[at, :] = b * s * (1.0 + a * (1.0 - s))
        up_f[at, :] = a * s

    @pl.loop(0, side)
    def _(s):
        i = lax.broadcasted_iota(jnp.int32, (block, 1), 0)
        swapped = (i // cap) * block + s * cap + i % cap
        straight = s * block + i
        target = swapped + core * (straight - swapped)
        lane = lax.broadcasted_iota(jnp.int32, (block, slots), 1)
        order[pl.ds(pl.multiple_of(s * block, block), block), :] = jnp.where(
            lane == target, 1.0, 0.0
        ).astype(BF16)

    loads[2].wait()
    exchange_wait(msg_out, msg_in, a2a_send, a2a_recv)

    tile = min(256, slots)
    tiles = slots // tile

    @pl.loop(0, tiles)
    def _(i):
        at = pl.ds(pl.multiple_of(i * tile, tile), tile)
        rows[:, at] = jnp.dot(msg_in[...], order[:, at], preferred_element_type=F32).astype(BF16)

    def sib_copy(i):
        at = pl.ds(pl.multiple_of(i * tile, tile), tile)
        return pltpu.make_async_remote_copy(
            src_ref=sib_out.at[:, at],
            dst_ref=sib_in.at[:, at],
            send_sem=sib_send.at[i],
            recv_sem=sib_recv.at[i],
            device_id=sibling,
            device_id_type=MESH,
        )

    mine = pl.ds(pl.multiple_of(core * half_hid, half_hid), half_hid)
    other = pl.ds(pl.multiple_of((1 - core) * half_hid, half_hid), half_hid)

    @pl.loop(0, tiles)
    def _(i):
        at = pl.ds(pl.multiple_of(i * tile, tile), tile)
        sib_out[:, at] = jnp.dot(
            wd_v[other, :], rows[pl.ds(0, feats), at], preferred_element_type=F32
        ).astype(BF16)
        sib_copy(i).start()

    @pl.loop(0, tiles)
    def _(i):
        at = pl.ds(pl.multiple_of(i * tile, tile), tile)
        total = jnp.dot(wd_v[mine, :], rows[pl.ds(0, feats), at], preferred_element_type=F32)
        sib_copy(i).wait()
        acc[:, at] = total + sib_in[:, at].astype(F32)

    def z_term(owner, half):
        return acc[
            pl.ds(pl.multiple_of(owner * chunk, chunk), chunk), pl.ds(half * half_slots, half_slots)
        ]

    def raw_view(which_core, owner, half):
        at = pl.ds(pl.multiple_of(which_core * half_hid + owner * chunk, chunk), chunk)
        return raw.at[at, pl.ds(half * half_slots, half_slots)]

    sums, more = ring_sum(z, depth, at_z, z_term, zs_out, zs_in, zs_send, zs_recv)
    sent += more

    def to_sibling(which_core, owner, half, sem):
        place = raw_view(which_core, owner, half)
        return pltpu.make_async_remote_copy(
            src_ref=place,
            dst_ref=place,
            send_sem=sg_send.at[sem],
            recv_sem=sg_recv.at[sem],
            device_id=sibling,
            device_id_type=MESH,
        )

    expected = []

    def pass_on(owner, half, sem):
        going = to_sibling(core, owner, half, sem)
        going.start()
        sent.append(going)
        expected.append((owner, half, sem))

    for half in range(2):
        at = pl.ds(pl.multiple_of(core * half_hid + z * chunk, chunk), chunk)
        raw[at, pl.ds(half * half_slots, half_slots)] = sums[half].astype(BF16)

    sent += ring_gather(
        z,
        depth,
        at_z,
        lambda owner, half: raw_view(core, owner, half),
        zg_send,
        zg_recv,
        lambda stream, step, owner, half: pass_on(owner, half, 2 + stream * (depth // 2) + step),
    )
    for half in range(2):
        pass_on(z, half, half)
    for owner, half, sem in expected:
        to_sibling(1 - core, owner, half, sem).wait_recv()

    loads[3].wait()
    loads[4].wait()
    head = rows[pl.ds(feats, HEAD), :].astype(F32)
    weight = jnp.sum(
        jnp.where(head[4:8] == group.astype(F32), head[0:4], 0.0), axis=0, keepdims=True
    )
    acc[pl.ds(0, 8), :] = jnp.broadcast_to(weight, (8, slots))

    @pl.loop(0, tiles)
    def _(i):
        at = pl.ds(pl.multiple_of(i * tile, tile), tile)
        hid = raw[:, at].astype(F32) * acc[pl.ds(0, 1), at]
        gate_grad = (hid * gate_f[:, at]).astype(BF16)
        up_grad = (hid * up_f[:, at]).astype(BF16)
        total = jnp.dot(wg_v[...], gate_grad, preferred_element_type=F32)
        total = total + jnp.dot(wu_v[...], up_grad, preferred_element_type=F32)
        grad[:, at] = total.astype(BF16)

    exchange_start(grad, order, ret_out, ret_in, ret_send, ret_recv)
    exchange_wait(ret_out, ret_in, ret_send, ret_recv)

    @pl.loop(0, tiles)
    def _(i):
        at = pl.ds(pl.multiple_of(i * tile, tile), tile)
        part[:, at] = jnp.dot(ret_in[...], picks[:, at], preferred_element_type=F32)

    half_feats = feats // 2

    def tok_term(owner, half):
        return part[
            pl.ds(half * half_feats, half_feats),
            pl.ds(pl.multiple_of(owner * tokens, tokens), tokens),
        ]

    sums, more = ring_sum(first, side, at_first, tok_term, fs_out, fs_in, fs_send, fs_recv)
    sent += more
    for half in range(2):
        out_ref[pl.ds(half * half_feats, half_feats), :] = sums[half].astype(BF16)
    for going in sent:
        going.wait_send()


def shards(side, depth, out_grad, groups, slots, drops, combine, gate, up, wg, wu, wd):
    tokens, feats = out_grad.shape
    hidden, places = gate.shape[1:]
    cap = places // (side * side)
    kept = jnp.where(drops == 0, groups, -1)
    ext = jnp.concatenate(
        [
            out_grad.T,
            combine.T,
            kept.astype(BF16).T,
            slots.astype(BF16).T,
            jnp.zeros((HEAD - 12, tokens), BF16),
        ],
        axis=0,
    )
    high = feats + HEAD
    half_hid, half_feats = hidden // 2, feats // 2
    width = side * tokens
    ring, line = max(side // 2, 1), max(depth // 2, 1)
    chunk, half_places = half_hid // depth, places // 2
    tiles = places // min(256, places)
    dma = pltpu.SemaphoreType.DMA
    scratch = [
        pltpu.VMEM((hidden, places), BF16),
        pltpu.VMEM((hidden, places), BF16),
        pltpu.VMEM((feats, hidden), BF16),
        pltpu.VMEM((feats, hidden), BF16),
        pltpu.VMEM((hidden, feats), BF16),
        pltpu.VMEM((hidden, places), F32),
        pltpu.VMEM((hidden, places), F32),
        pltpu.VMEM((high, width), BF16),
        pltpu.VMEM((places, width), BF16),
        pltpu.VMEM((places, places), BF16),
        pltpu.VMEM((high, places), BF16),
        pltpu.VMEM((high, places), BF16),
        pltpu.VMEM((high, places), BF16),
        pltpu.VMEM((half_hid, places), BF16),
        pltpu.VMEM((half_hid, places), BF16),
        pltpu.VMEM((half_hid, places), F32),
        pltpu.VMEM((4, line, chunk, half_places), BF16),
        pltpu.VMEM((4, line, chunk, half_places), BF16),
        pltpu.VMEM((hidden, places), BF16),
        pltpu.VMEM((feats, places), BF16),
        pltpu.VMEM((feats, places), BF16),
        pltpu.VMEM((feats, places), BF16),
        pltpu.VMEM((feats, width), F32),
        pltpu.VMEM((4, ring, half_feats, tokens), BF16),
        pltpu.VMEM((4, ring, half_feats, tokens), BF16),
        dma((5,)),
        dma((4, ring)),
        dma((4, ring)),
        dma((side,)),
        dma((side,)),
        dma((tiles,)),
        dma((tiles,)),
        dma((4, line)),
        dma((4, line)),
        dma((4, line)),
        dma((4, line)),
        dma((2 + 4 * line,)),
        dma((2 + 4 * line,)),
        dma((side,)),
        dma((side,)),
        dma((4, ring)),
        dma((4, ring)),
    ]
    vmem, hbm = pl.BlockSpec(memory_space=pltpu.VMEM), pl.BlockSpec(memory_space=pl.ANY)
    columns = pl.pallas_call(
        functools.partial(kernel, side, depth, cap),
        out_shape=jax.ShapeDtypeStruct((feats, tokens), BF16),
        in_specs=[vmem] + [hbm] * 5,
        out_specs=vmem,
        scratch_shapes=scratch,
        compiler_params=pltpu.CompilerParams(
            collective_id=0, has_side_effects=True, vmem_limit_bytes=56 * 2**20
        ),
    )(ext, gate[0], up[0], wg[0], wu[0], wd[0])
    return columns.T


def solution(mesh):
    placed = (
        P("group", "local"),
        P("group", None),
        P("group", None),
        P("group", None),
        P("group", None),
        P("group", None, None),
        P("group", None, None),
        P("group", "local", None),
        P("group", "local", None),
        P("group", None, "local"),
    )
    side = math.isqrt(mesh.shape["group"])
    depth = mesh.shape["local"] // 2
    return jax.shard_map(
        functools.partial(shards, side, depth),
        mesh=mesh,
        in_specs=placed,
        out_specs=P("group", "local"),
        check_vma=False,
    )
```

time: 249 us -> 134 us (0.54); the launches traced: 245 us -> 133 us
  Pallas kernels: 0 us -> 125 us
  waiting for transfers between devices: 119 us -> 0 us
  blocking collectives: 75.5 us -> 0 us
  between operations: 13.5 us -> 0.01 us
  matrix products: 13 us -> 0 us
  starting transfers between devices: 11.3 us -> 0 us
  local copies, waits for them, and re-layouts: 10.1 us -> 7.23 us
    pallas_call x0 -> x1, Pallas kernels: none -> 125 us  [shards(): pl.pallas_call(functools.partial(kernel, side, depth, cap), out_shape=jax...]
    psum x1 -> x0, waiting for transfers between devices: 115 us -> none  [shards(): lax.psum(partial_sums.astype(jnp.bfloat16), 'local').astype(jnp.float32)]
    all_to_all x2 -> x0, blocking collectives: 75.5 us -> none  [the longest x1 38.5 us: shards(): lax.all_to_all(slot_grad.reshape(groups_count, capacity, feature_cols), '...]
    dot_general x5 -> x0, matrix products: 13 us -> none  [the longest x1 5.11 us: shards(): jnp.einsum('hs,dh->sd', gate_grad, gate_weights, preferred_element_type=j...]
    all_to_all x1 -> x0, starting transfers between devices: 11.3 us -> none  [shards(): lax.all_to_all(weight_col.reshape(groups_count, capacity), 'group', split...]
    all_to_all x1 -> x0, waiting for transfers between devices: 4.07 us -> none  [shards(): lax.all_to_all(weight_col.reshape(groups_count, capacity), 'group', split...]
    unnamed x14 -> x2, local copies, waits for them, and re-layouts: 7.36 us -> 3.81 us
    concatenate x0 -> x1, local copies, waits for them, and re-layouts: none -> 3.42 us  [shards(): jnp.concatenate([out_grad.T, combine.T, kept.astype(BF16).T, slots.astype...]
  transfers between devices with their start and end apart: 2 -> 0, of which waited for: 2 -> 0; matrix products, arithmetic and copies ran while one was open for 3% -> 0% of each run, Pallas kernels for 0% -> 0%
where the time goes in v1:
time: 134 us; the launch traced here: 133 us
  Pallas kernels  125 us (93%)
  local copies, waits for them, and re-layouts  7.23 us (5%)
    pallas_call x1, Pallas kernels, shards(): pl.pallas_call(functools.partial(kernel, side, depth, cap), out_shape=jax...  125 us
    unnamed x2, local copies, waits for them, and re-layouts  3.81 us
    concatenate x1, local copies, waits for them, and re-layouts, shards(): jnp.concatenate([out_grad.T, combine.T, kept.astype(BF16).T, slots.astype...  3.42 us

profile of v1, /device:TPU:1, one launch (start us, length us, event | category | flops | bytes accessed | tf_op | source)
XLA Modules:
  0.0 132.7 jit_solution(4119873085549310189)
XLA Ops:
  0.0 0.7 fusion
  0.7 3.4 %concatenate.3.ext_ref = bf16[464,128]{1,0:T(8,128)(2,1)} concatenate(bf16[448,128]{1,0:T(8,128)(2,1)} %bitcast.18, bf16[4,128]{1,0:T(4,128)(2,1)} %bitcast.19, bf16[4,128]{1,0:T(4,128)(2,1)S(1)} %get-tuple-element.5, bf16[4,128]{1,0:T(4,128)(2,1)S(1)} %get-tuple-element.6, bf16[4,128]{1,0:T(4,128)(2,1)S(1)} %broadcast_in_dim.8), dimensions={0} | concatenate | bytes 237568 | tf_op jit(solution)/shard_map/concatenate | solution.py:409
  4.1 2.3 %copy.11 = bf16[1,1024,448]{2,1,0:T(8,128)(2,1)} copy(bf16[1,1024,448]{1,2,0:T(8,128)(2,1)} %param.19) | data formatting | bytes 1835008 | tf_op args[9]
  6.4 124.8 %shard_map.100 = bf16[448,128]{1,0:T(8,128)(2,1)} custom-call(bf16[464,128]{1,0:T(8,128)(2,1)} %concatenate.3.ext_ref, bf16[1024,1024]{1,0:T(8,128)(2,1)} %bitcast.13, bf16[1024,1024]{1,0:T(8,128)(2,1)} %bitcast.14, bf16[448,1024]{1,0:T(8,128)(2,1)} %bitcast.15, bf16[448,1024]{1,0:T(8,128)(2,1)} %bitcast.16, bf16[1024,448]{1,0:T(8,128)(2,1)} %bitcast.12), custom_call_target="tpu_custom_call" | custom-call | tf_op jit(solution)/shard_map/pallas_call | solution.py:471
  131.2 1.6 %copy.13 = bf16[128,448]{0,1:T(8,128)(2,1)} copy(bf16[128,448]{0,1:T(8,128)(2,1)} %bitcast.17) | data formatting | bytes 229376
  (1 shorter events, 0.0 us)

commit v2 on v1

v2 whole, which is shorter than its diff:
```python
import functools
import math

import jax
import jax.numpy as jnp
from jax import lax
from jax.experimental import pallas as pl
from jax.experimental.pallas import tpu as pltpu
from jax.sharding import PartitionSpec as P

MESH = pl.DeviceIdType.MESH
F32 = jnp.float32
BF16 = jnp.bfloat16
HEAD = 16


PIECES = 4


def streams(n):
    long, short = n // 2, max(n // 2 - 1, 0)
    pairs = [(sign, piece) for piece in range(PIECES) for sign in (1, -1)]
    return [
        (sign, piece, long if (sign == 1) == (piece % 2 == 0) else short) for sign, piece in pairs
    ]


def ring_gather(pos, n, device, view, send_sem, recv_sem, landed=None):
    def copy(stream, step, owner):
        sign, piece, _ = streams(n)[stream]
        place = view(owner, piece)
        return pltpu.make_async_remote_copy(
            src_ref=place,
            dst_ref=place,
            send_sem=send_sem.at[stream, step],
            recv_sem=recv_sem.at[stream, step],
            device_id=device(lax.rem(pos + sign + n, n)),
            device_id_type=MESH,
        )

    def owner_of(sign, step):
        return lax.rem(pos - sign * step + n, n)

    sent = []
    for step in range(n // 2 + 1):
        for stream, (sign, piece, steps) in enumerate(streams(n)):
            if 0 < step <= steps:
                owner = owner_of(sign, step)
                copy(stream, step - 1, owner).wait_recv()
            if step < steps:
                going = copy(stream, step, owner_of(sign, step))
                going.start()
                sent.append(going)
            if 0 < step <= steps and landed is not None:
                landed(stream, step - 1, owner, piece)
    return sent


def ring_sum(pos, n, device, prepare, term, out_buf, in_buf, send_sem, recv_sem):
    def copy(stream, step):
        sign = streams(n)[stream][0]
        return pltpu.make_async_remote_copy(
            src_ref=out_buf.at[stream, step],
            dst_ref=in_buf.at[stream, step],
            send_sem=send_sem.at[stream, step],
            recv_sem=recv_sem.at[stream, step],
            device_id=device(lax.rem(pos + sign + n, n)),
            device_id_type=MESH,
        )

    sent = []
    for step in range(max(n // 2, 1)):
        for stream, (sign, piece, steps) in enumerate(streams(n)):
            if step == 0 and sign == 1:
                prepare(piece)
            if step >= steps:
                continue
            value = term(lax.rem(pos + sign * (steps - step) + n, n), piece)
            if step > 0:
                copy(stream, step - 1).wait_recv()
                value = value + in_buf[stream, step - 1].astype(F32)
            out_buf[stream, step] = value.astype(BF16)
            going = copy(stream, step)
            going.start()
            sent.append(going)
    sums = []
    for piece in range(PIECES):
        value = term(pos, piece)
        for stream, (sign, which, steps) in enumerate(streams(n)):
            if which == piece and steps > 0:
                copy(stream, steps - 1).wait_recv()
                value = value + in_buf[stream, steps - 1].astype(F32)
        sums.append(value)
    return sums, sent


def kernel(
    side,
    depth,
    cap,
    grad_ref,
    groups_ref,
    slots_ref,
    drops_ref,
    combine_ref,
    gate_hbm,
    up_hbm,
    wg_hbm,
    wu_hbm,
    wd_hbm,
    out_ref,
    gate_v,
    up_v,
    wg_v,
    wu_v,
    wd_soon,
    wd_late,
    wdt_v,
    gate_f,
    up_f,
    toks,
    picks,
    order,
    msg_out,
    msg_in,
    rows,
    sib_out,
    sib_in,
    acc,
    theirs,
    zs_out,
    zs_in,
    raw,
    grad,
    ret_out,
    ret_in,
    fs_out,
    fs_in,
    load_sem,
    tg_send,
    tg_recv,
    a2a_send,
    a2a_recv,
    sib_send,
    sib_recv,
    zs_send,
    zs_recv,
    zg_send,
    zg_recv,
    sg_send,
    sg_recv,
    ret_send,
    ret_recv,
    fs_send,
    fs_recv,
):
    group, local = lax.axis_index("group"), lax.axis_index("local")
    core, z = lax.rem(local, 2), lax.div(local, 2)
    gx, gy = lax.div(group, side), lax.rem(group, side)
    first = gx + core * (gy - gx)
    second = gy + core * (gx - gy)
    first_step = side - core * (side - 1)
    second_step = 1 + core * (side - 1)
    sibling = (group, local + 1 - 2 * core)
    feats, tokens = grad_ref.shape
    slots = gate_v.shape[1]
    hidden = gate_v.shape[0]
    block = side * cap
    half_hid = hidden // 2
    chunk = half_hid // depth
    span = slots // PIECES

    def at_first(f):
        return (f * first_step + second * second_step, local)

    def at_second(s):
        return (first * first_step + s * second_step, local)

    def at_z(q):
        return (group, q * 2 + core)

    loads = [
        pltpu.make_async_copy(src, dst, load_sem.at[i])
        for i, (src, dst) in enumerate(
            ((gate_hbm, gate_v), (up_hbm, up_v), (wd_hbm, wdt_v), (wg_hbm, wg_v), (wu_hbm, wu_v))
        )
    ]
    for load in loads:
        load.start()

    barrier = pltpu.get_barrier_semaphore()
    peers = [at_first(lax.rem(first + d, side)) for d in range(1, side)]
    peers += [at_second(lax.rem(second + d, side)) for d in range(1, side)]
    if depth > 1:
        peers += [at_z(lax.rem(z + 1, depth)), at_z(lax.rem(z + depth - 1, depth))]
    peers += [sibling]
    for peer in peers:
        pl.semaphore_signal(barrier, inc=1, device_id=peer, device_id_type=MESH)

    kept = jnp.where(drops_ref[...] == 0, groups_ref[...], -1).astype(F32)
    line = lax.broadcasted_iota(jnp.int32, (HEAD, tokens), 0)
    table = jnp.zeros((HEAD, tokens), F32)
    for i, values in enumerate((combine_ref[...].astype(F32), kept, slots_ref[...].astype(F32))):
        for j in range(4):
            table = jnp.where(line == 4 * i + j, values[j : j + 1], table)
    here = pl.ds(pl.multiple_of(first * tokens, tokens), tokens)
    toks[pl.ds(0, feats), here] = grad_ref[...]
    toks[pl.ds(feats, HEAD), here] = table.astype(BF16)
    pl.semaphore_wait(barrier, len(peers))

    cut = (feats // 32) * 16
    parts = (pl.ds(cut, feats - cut + HEAD), pl.ds(0, cut))
    back = (pl.ds(cut, feats - cut), pl.ds(0, cut))

    def tok_copy(d, part):
        return pltpu.make_async_remote_copy(
            src_ref=toks.at[parts[part], here],
            dst_ref=toks.at[parts[part], here],
            send_sem=tg_send.at[part, d],
            recv_sem=tg_recv.at[part, d],
            device_id=at_first(lax.rem(first + d, side)),
            device_id_type=MESH,
        )

    sent = []
    for part in range(2):
        for d in range(1, side):
            going = tok_copy(d, part)
            going.start()
            sent.append(going)
    picks[...] = jnp.zeros_like(picks)
    for d in range(1, side):
        tok_copy(d, 0).wait_recv()

    @pl.loop(0, side)
    def _(f):
        lanes = pl.ds(pl.multiple_of(f * tokens, tokens), tokens)
        table = toks[pl.ds(feats, HEAD), lanes].astype(F32)
        place = table[4:8] * cap + table[8:12]
        slot = lax.broadcasted_iota(jnp.int32, (cap, tokens), 0)
        for e in range(side):
            wanted = ((first * first_step + e * second_step) * cap + slot).astype(F32)
            hit = wanted == place[0:1]
            for j in range(1, 4):
                hit = hit | (wanted == place[j : j + 1])
            at = pl.ds(pl.multiple_of(e * block + f * cap, cap), cap)
            picks[at, lanes] = jnp.where(hit, 1.0, 0.0).astype(BF16)

    def exchange_copy(d, span, part, out_buf, in_buf, send_sem, recv_sem):
        return pltpu.make_async_remote_copy(
            src_ref=out_buf.at[span, pl.ds(pl.multiple_of(d * block, block), block)],
            dst_ref=in_buf.at[span, pl.ds(pl.multiple_of(second * block, block), block)],
            send_sem=send_sem.at[part, d],
            recv_sem=recv_sem.at[part, d],
            device_id=at_second(lax.rem(second + d, side)),
            device_id_type=MESH,
        )

    def exchange_start(left, matrix, span, part, out_buf, in_buf, send_sem, recv_sem):
        @pl.loop(0, side)
        def _(i):
            d = lax.rem(i + side // 2, side)
            e = lax.rem(second + d, side)
            picked = matrix[pl.ds(pl.multiple_of(e * block, block), block), :]
            message = lax.dot_general(
                left[span, :], picked, (((1,), (1,)), ((), ())), preferred_element_type=F32
            ).astype(BF16)

            @pl.when(d == 0)
            def _():
                in_buf[span, pl.ds(pl.multiple_of(second * block, block), block)] = message

            @pl.when(d != 0)
            def _():
                out_buf[span, pl.ds(pl.multiple_of(d * block, block), block)] = message
                exchange_copy(d, span, part, out_buf, in_buf, send_sem, recv_sem).start()

    def exchange_wait(span, part, out_buf, in_buf, send_sem, recv_sem):
        @pl.loop(1, side)
        def _(d):
            exchange_copy(d, span, part, out_buf, in_buf, send_sem, recv_sem).wait()

    exchange_start(toks, picks, parts[0], 0, msg_out, msg_in, a2a_send, a2a_recv)
    for d in range(1, side):
        tok_copy(d, 1).wait_recv()
    exchange_start(toks, picks, parts[1], 1, msg_out, msg_in, a2a_send, a2a_recv)

    loads[0].wait()
    loads[1].wait()
    strip = 16

    @pl.loop(0, hidden // strip)
    def _(i):
        at = pl.ds(pl.multiple_of(i * strip, strip), strip)
        a = gate_v[at, :].astype(F32)
        b = up_v[at, :].astype(F32)
        s = jax.nn.sigmoid(a)
        gate_f[at, :] = b * s * (1.0 + a * (1.0 - s))
        up_f[at, :] = a * s

    @pl.loop(0, side)
    def _(s):
        i = lax.broadcasted_iota(jnp.int32, (block, 1), 0)
        swapped = (i // cap) * block + s * cap + i % cap
        straight = s * block + i
        target = swapped + core * (straight - swapped)
        lane = lax.broadcasted_iota(jnp.int32, (block, slots), 1)
        order[pl.ds(pl.multiple_of(s * block, block), block), :] = jnp.where(
            lane == target, 1.0, 0.0
        ).astype(BF16)

    loads[2].wait()
    turn = min(256, hidden)
    eye = jnp.where(
        lax.broadcasted_iota(jnp.int32, (turn, turn), 0)
        == lax.broadcasted_iota(jnp.int32, (turn, turn), 1),
        1.0,
        0.0,
    ).astype(BF16)

    @pl.loop(0, hidden // turn)
    def _(i):
        at = pl.ds(pl.multiple_of(i * turn, turn), turn)
        for part in range(2):
            (wd_late, wd_soon)[1 - part][at, :] = lax.dot_general(
                eye, wdt_v[back[part], at], (((1,), (1,)), ((), ())), preferred_element_type=F32
            ).astype(BF16)

    tile = min(256, slots // PIECES)
    tiles = slots // tile
    mine = pl.ds(pl.multiple_of(core * half_hid, half_hid), half_hid)
    other = pl.ds(pl.multiple_of((1 - core) * half_hid, half_hid), half_hid)

    def sort_rows(part, at):
        rows[parts[part], at] = jnp.dot(
            msg_in[parts[part], :], order[:, at], preferred_element_type=F32
        ).astype(BF16)

    def product(part, hid, at):
        return jnp.dot(
            (wd_soon, wd_late)[part][hid, :], rows[back[part], at], preferred_element_type=F32
        )

    exchange_wait(parts[0], 0, msg_out, msg_in, a2a_send, a2a_recv)

    @pl.loop(0, tiles)
    def _(i):
        at = pl.ds(pl.multiple_of(i * tile, tile), tile)
        sort_rows(0, at)
        theirs[:, at] = product(0, other, at)
        acc[:, at] = product(0, mine, at)

    def sib_copy(i):
        at = pl.ds(pl.multiple_of(i * tile, tile), tile)
        return pltpu.make_async_remote_copy(
            src_ref=sib_out.at[:, at],
            dst_ref=sib_in.at[:, at],
            send_sem=sib_send.at[i],
            recv_sem=sib_recv.at[i],
            device_id=sibling,
            device_id_type=MESH,
        )

    exchange_wait(parts[1], 1, msg_out, msg_in, a2a_send, a2a_recv)

    @pl.loop(0, tiles)
    def _(i):
        at = pl.ds(pl.multiple_of(i * tile, tile), tile)
        sort_rows(1, at)
        sib_out[:, at] = (theirs[:, at] + product(1, other, at)).astype(BF16)
        sib_copy(i).start()

    def own_piece(piece):
        @pl.loop(piece * (tiles // PIECES), (piece + 1) * (tiles // PIECES))
        def _(i):
            at = pl.ds(pl.multiple_of(i * tile, tile), tile)
            total = acc[:, at] + product(1, mine, at)
            sib_copy(i).wait()
            acc[:, at] = total + sib_in[:, at].astype(F32)

    def z_term(owner, piece):
        return acc[
            pl.ds(pl.multiple_of(owner * chunk, chunk), chunk), pl.ds(piece * span, span)
        ]

    def raw_view(which_core, owner, piece):
        at = pl.ds(pl.multiple_of(which_core * half_hid + owner * chunk, chunk), chunk)
        return raw.at[at, pl.ds(piece * span, span)]

    sums, more = ring_sum(z, depth, at_z, own_piece, z_term, zs_out, zs_in, zs_send, zs_recv)
    sent += more

    def to_sibling(which_core, owner, piece, sem):
        place = raw_view(which_core, owner, piece)
        return pltpu.make_async_remote_copy(
            src_ref=place,
            dst_ref=place,
            send_sem=sg_send.at[sem],
            recv_sem=sg_recv.at[sem],
            device_id=sibling,
            device_id_type=MESH,
        )

    expected = []

    def pass_on(owner, piece, sem):
        going = to_sibling(core, owner, piece, sem)
        going.start()
        sent.append(going)
        expected.append((owner, piece, sem))

    for piece in range(PIECES):
        at = pl.ds(pl.multiple_of(core * half_hid + z * chunk, chunk), chunk)
        raw[at, pl.ds(piece * span, span)] = sums[piece].astype(BF16)

    sent += ring_gather(
        z,
        depth,
        at_z,
        lambda owner, piece: raw_view(core, owner, piece),
        zg_send,
        zg_recv,
        lambda stream, step, owner, piece: pass_on(owner, piece, PIECES + stream * max(depth // 2, 1) + step),
    )
    for piece in range(PIECES):
        pass_on(z, piece, piece)
    for owner, piece, sem in expected:
        to_sibling(1 - core, owner, piece, sem).wait_recv()

    loads[3].wait()
    loads[4].wait()
    head = rows[pl.ds(feats, HEAD), :].astype(F32)
    weight = jnp.sum(
        jnp.where(head[4:8] == group.astype(F32), head[0:4], 0.0), axis=0, keepdims=True
    )
    acc[pl.ds(0, 8), :] = jnp.broadcast_to(weight, (8, slots))

    def grads(part, gate_grad, up_grad):
        total = jnp.dot(wg_v[back[part], :], gate_grad, preferred_element_type=F32)
        total = total + jnp.dot(wu_v[back[part], :], up_grad, preferred_element_type=F32)
        return total.astype(BF16)

    @pl.loop(0, tiles)
    def _(i):
        at = pl.ds(pl.multiple_of(i * tile, tile), tile)
        hid = raw[:, at].astype(F32) * acc[pl.ds(0, 1), at]
        gate_grad = (hid * gate_f[:, at]).astype(BF16)
        up_grad = (hid * up_f[:, at]).astype(BF16)
        gate_v[:, at] = gate_grad
        up_v[:, at] = up_grad
        grad[back[0], at] = grads(0, gate_grad, up_grad)

    exchange_start(grad, order, back[0], 0, ret_out, ret_in, ret_send, ret_recv)

    @pl.loop(0, tiles)
    def _(i):
        at = pl.ds(pl.multiple_of(i * tile, tile), tile)
        grad[back[1], at] = grads(1, gate_v[:, at], up_v[:, at])

    exchange_start(grad, order, back[1], 1, ret_out, ret_in, ret_send, ret_recv)

    def sum_copy(d, part):
        return pltpu.make_async_remote_copy(
            src_ref=fs_out.at[back[part], pl.ds(pl.multiple_of(d * tokens, tokens), tokens)],
            dst_ref=fs_in.at[back[part], here],
            send_sem=fs_send.at[part, d],
            recv_sem=fs_recv.at[part, d],
            device_id=at_first(lax.rem(first + d, side)),
            device_id_type=MESH,
        )

    def sum_start(part):
        @pl.loop(0, side)
        def _(i):
            d = lax.rem(i + side // 2, side)
            f = lax.rem(first + d, side)
            partial = jnp.dot(
                ret_in[back[part], :],
                picks[:, pl.ds(pl.multiple_of(f * tokens, tokens), tokens)],
                preferred_element_type=F32,
            ).astype(BF16)

            @pl.when(d == 0)
            def _():
                fs_in[back[part], here] = partial

            @pl.when(d != 0)
            def _():
                fs_out[back[part], pl.ds(pl.multiple_of(d * tokens, tokens), tokens)] = partial
                sum_copy(d, part).start()

    for part in range(2):
        exchange_wait(back[part], part, ret_out, ret_in, ret_send, ret_recv)
        sum_start(part)
    for part in range(2):

        @pl.loop(1, side)
        def _(d):
            sum_copy(d, part).wait()

    total = fs_in[:, pl.ds(0, tokens)].astype(F32)
    for f in range(1, side):
        total = total + fs_in[:, pl.ds(f * tokens, tokens)].astype(F32)
    out_ref[...] = total.astype(BF16)
    for going in sent:
        going.wait_send()


def shards(side, depth, out_grad, groups, slots, drops, combine, gate, up, wg, wu, wd):
    tokens, feats = out_grad.shape
    hidden, places = gate.shape[1:]
    cap = places // (side * side)
    high = feats + HEAD
    half_hid = hidden // 2
    width = side * tokens
    line = max(depth // 2, 1)
    chunk, span = half_hid // depth, places // PIECES
    tiles = places // min(256, places // PIECES)
    dma = pltpu.SemaphoreType.DMA
    scratch = [
        pltpu.VMEM((hidden, places), BF16),
        pltpu.VMEM((hidden, places), BF16),
        pltpu.VMEM((feats, hidden), BF16),
        pltpu.VMEM((feats, hidden), BF16),
        pltpu.VMEM((hidden, feats - feats // 32 * 16), BF16),
        pltpu.VMEM((hidden, feats // 32 * 16), BF16),
        pltpu.VMEM((feats, hidden), BF16),
        pltpu.VMEM((hidden, places), F32),
        pltpu.VMEM((hidden, places), F32),
        pltpu.VMEM((high, width), BF16),
        pltpu.VMEM((places, width), BF16),
        pltpu.VMEM((places, places), BF16),
        pltpu.VMEM((high, places), BF16),
        pltpu.VMEM((high, places), BF16),
        pltpu.VMEM((high, places), BF16),
        pltpu.VMEM((half_hid, places), BF16),
        pltpu.VMEM((half_hid, places), BF16),
        pltpu.VMEM((half_hid, places), F32),
        pltpu.VMEM((half_hid, places), F32),
        pltpu.VMEM((2 * PIECES, line, chunk, span), BF16),
        pltpu.VMEM((2 * PIECES, line, chunk, span), BF16),
        pltpu.VMEM((hidden, places), BF16),
        pltpu.VMEM((feats, places), BF16),
        pltpu.VMEM((feats, places), BF16),
        pltpu.VMEM((feats, places), BF16),
        pltpu.VMEM((feats, width), BF16),
        pltpu.VMEM((feats, width), BF16),
        dma((5,)),
        dma((2, side)),
        dma((2, side)),
        dma((2, side)),
        dma((2, side)),
        dma((tiles,)),
        dma((tiles,)),
        dma((2 * PIECES, line)),
        dma((2 * PIECES, line)),
        dma((2 * PIECES, line)),
        dma((2 * PIECES, line)),
        dma((PIECES + 2 * PIECES * line,)),
        dma((PIECES + 2 * PIECES * line,)),
        dma((2, side)),
        dma((2, side)),
        dma((2, side)),
        dma((2, side)),
    ]
    vmem, hbm = pl.BlockSpec(memory_space=pltpu.VMEM), pl.BlockSpec(memory_space=pl.ANY)
    columns = pl.pallas_call(
        functools.partial(kernel, side, depth, cap),
        out_shape=jax.ShapeDtypeStruct((feats, tokens), BF16),
        in_specs=[vmem] * 5 + [hbm] * 5,
        out_specs=vmem,
        scratch_shapes=scratch,
        compiler_params=pltpu.CompilerParams(
            collective_id=0, has_side_effects=True, vmem_limit_bytes=56 * 2**20
        ),
    )(
        out_grad.T,
        groups.T,
        slots.T,
        drops.T,
        combine.T,
        gate[0],
        up[0],
        wg[0],
        wu[0],
        wd[0].T,
    )
    return columns.T


def solution(mesh):
    placed = (
        P("group", "local"),
        P("group", None),
        P("group", None),
        P("group", None),
        P("group", None),
        P("group", None, None),
        P("group", None, None),
        P("group", "local", None),
        P("group", "local", None),
        P("group", None, "local"),
    )
    side = math.isqrt(mesh.shape["group"])
    depth = mesh.shape["local"] // 2
    return jax.shard_map(
        functools.partial(shards, side, depth),
        mesh=mesh,
        in_specs=placed,
        out_specs=P("group", "local"),
        check_vma=False,
    )
```

time: 134 us -> 118 us (0.88)
  Pallas kernels: 125 us -> 116 us
  local copies, waits for them, and re-layouts: 7.23 us -> 1.55 us
    pallas_call x1, Pallas kernels: 125 us -> 116 us  [shards(): pl.pallas_call(functools.partial(kernel, side, depth, cap), out_shape=jax...]
    concatenate x1 -> x0, local copies, waits for them, and re-layouts: 3.42 us -> none  [shards(): jnp.concatenate([out_grad.T, combine.T, kept.astype(BF16).T, slots.astype...]
    unnamed x2 -> x1, local copies, waits for them, and re-layouts: 3.81 us -> 1.55 us
where the time goes in v2:
time: 118 us
  Pallas kernels  116 us (98%)
  local copies, waits for them, and re-layouts  1.55 us (1%)
    pallas_call x1, Pallas kernels, shards(): pl.pallas_call(functools.partial(kernel, side, depth, cap), out_shape=jax...  116 us

profile of v2, /device:TPU:1, one launch (start us, length us, event | category | flops | bytes accessed | tf_op | source)
XLA Modules:
  0.0 118.0 jit_solution(17651691377892637374)
XLA Ops:
  0.0 116.5 %shard_map.100 = bf16[448,128]{1,0:T(8,128)(2,1)} custom-call(bf16[448,128]{1,0:T(8,128)(2,1)} %bitcast.19, s32[4,128]{1,0:T(4,128)} %bitcast.20, s32[4,128]{1,0:T(4,128)} %bitcast.21, s32[4,128]{1,0:T(4,128)} %bitcast.22, bf16[4,128]{1,0:T(4,128)(2,1)} %bitcast.23, bf16[1024,1024]{1,0:T(8,128)(2,1)} %bitcast.13, bf16[1024,1024]{1,0:T(8,128)(2,1)} %bitcast.14, ...), custom_call_target="tpu_custom_call" | custom-call | tf_op jit(solution)/shard_map/pallas_call | solution.py:567
  116.5 1.6 %copy.12 = bf16[128,448]{0,1:T(8,128)(2,1)} copy(bf16[128,448]{0,1:T(8,128)(2,1)} %bitcast.18) | data formatting | bytes 229376

commit v3 on v2

--- a/solution.py
+++ b/solution.py
@@ -17,15 +17,20 @@
 PIECES = 4
 
 
+def late_feats(feats):
+    return feats // 3 // 16 * 16
+
+
 def streams(n):
     long, short = n // 2, max(n // 2 - 1, 0)
-    pairs = [(sign, piece) for piece in range(PIECES) for sign in (1, -1)]
-    return [
-        (sign, piece, long if (sign == 1) == (piece % 2 == 0) else short) for sign, piece in pairs
-    ]
-
-
-def ring_gather(pos, n, device, view, send_sem, recv_sem, landed=None):
+    ways = [1 - 2 * (piece % 2) for piece in range(PIECES)]
+    first = [(way, piece, long) for piece, way in enumerate(ways)]
+    return first + [(-way, piece, short) for piece, way in enumerate(ways)]
+
+
+def ring_gather(pos, n, device, view, send_sem, recv_sem, landed):
+    sent = []
+
     def copy(stream, step, owner):
         sign, piece, _ = streams(n)[stream]
         place = view(owner, piece)
@@ -41,22 +46,31 @@
     def owner_of(sign, step):
         return lax.rem(pos - sign * step + n, n)
 
-    sent = []
-    for step in range(n // 2 + 1):
-        for stream, (sign, piece, steps) in enumerate(streams(n)):
-            if 0 < step <= steps:
-                owner = owner_of(sign, step)
-                copy(stream, step - 1, owner).wait_recv()
-            if step < steps:
-                going = copy(stream, step, owner_of(sign, step))
-                going.start()
-                sent.append(going)
-            if 0 < step <= steps and landed is not None:
-                landed(stream, step - 1, owner, piece)
-    return sent
-
-
-def ring_sum(pos, n, device, prepare, term, out_buf, in_buf, send_sem, recv_sem):
+    def send(stream, step, owner):
+        going = copy(stream, step, owner)
+        going.start()
+        sent.append(going)
+
+    def start(piece):
+        for stream, (_, which, steps) in enumerate(streams(n)):
+            if which == piece and steps > 0:
+                send(stream, 0, pos)
+
+    def rest():
+        for step in range(1, n // 2 + 1):
+            for stream, (sign, piece, steps) in enumerate(streams(n)):
+                if step <= steps:
+                    owner = owner_of(sign, step)
+                    copy(stream, step - 1, owner).wait_recv()
+                    if step < steps:
+                        send(stream, step, owner)
+            for offset in sorted({step, n - step}):
+                landed(offset)
+
+    return sent, start, rest
+
+
+def ring_sum(pos, n, device, prepare, term, out_buf, in_buf, send_sem, recv_sem, done):
     def copy(stream, step):
         sign = streams(n)[stream][0]
         return pltpu.make_async_remote_copy(
@@ -71,7 +85,7 @@
     sent = []
     for step in range(max(n // 2, 1)):
         for stream, (sign, piece, steps) in enumerate(streams(n)):
-            if step == 0 and sign == 1:
+            if step == 0 and stream < PIECES:
                 prepare(piece)
             if step >= steps:
                 continue
@@ -83,15 +97,14 @@
             going = copy(stream, step)
             going.start()
             sent.append(going)
-    sums = []
     for piece in range(PIECES):
         value = term(pos, piece)
         for stream, (sign, which, steps) in enumerate(streams(n)):
             if which == piece and steps > 0:
                 copy(stream, steps - 1).wait_recv()
                 value = value + in_buf[stream, steps - 1].astype(F32)
-        sums.append(value)
-    return sums, sent
+        done(piece, value)
+    return sent
 
 
 def kernel(
@@ -136,6 +149,7 @@
     ret_in,
     fs_out,
     fs_in,
+    out_v,
     load_sem,
     tg_send,
     tg_recv,
@@ -153,6 +167,7 @@
     ret_recv,
     fs_send,
     fs_recv,
+    out_sem,
 ):
     group, local = lax.axis_index("group"), lax.axis_index("local")
     core, z = lax.rem(local, 2), lax.div(local, 2)
@@ -185,9 +200,6 @@
             ((gate_hbm, gate_v), (up_hbm, up_v), (wd_hbm, wdt_v), (wg_hbm, wg_v), (wu_hbm, wu_v))
         )
     ]
-    for load in loads:
-        load.start()
-
     barrier = pltpu.get_barrier_semaphore()
     peers = [at_first(lax.rem(first + d, side)) for d in range(1, side)]
     peers += [at_second(lax.rem(second + d, side)) for d in range(1, side)]
@@ -208,7 +220,7 @@
     toks[pl.ds(feats, HEAD), here] = table.astype(BF16)
     pl.semaphore_wait(barrier, len(peers))
 
-    cut = (feats // 32) * 16
+    cut = late_feats(feats)
     parts = (pl.ds(cut, feats - cut + HEAD), pl.ds(0, cut))
     back = (pl.ds(cut, feats - cut), pl.ds(0, cut))
 
@@ -223,11 +235,14 @@
         )
 
     sent = []
+    outward = sorted(range(1, side), key=lambda d: (abs(d - side // 2), d))
     for part in range(2):
-        for d in range(1, side):
+        for d in outward:
             going = tok_copy(d, part)
             going.start()
             sent.append(going)
+    for load in loads:
+        load.start()
     picks[...] = jnp.zeros_like(picks)
     for d in range(1, side):
         tok_copy(d, 0).wait_recv()
@@ -246,6 +261,9 @@
             at = pl.ds(pl.multiple_of(e * block + f * cap, cap), cap)
             picks[at, lanes] = jnp.where(hit, 1.0, 0.0).astype(BF16)
 
+    def turn_of(i):
+        return side // 2 + (1 - 2 * lax.rem(i, 2)) * lax.div(i + 1, 2)
+
     def exchange_copy(d, span, part, out_buf, in_buf, send_sem, recv_sem):
         return pltpu.make_async_remote_copy(
             src_ref=out_buf.at[span, pl.ds(pl.multiple_of(d * block, block), block)],
@@ -259,7 +277,7 @@
     def exchange_start(left, matrix, span, part, out_buf, in_buf, send_sem, recv_sem):
         @pl.loop(0, side)
         def _(i):
-            d = lax.rem(i + side // 2, side)
+            d = turn_of(i)
             e = lax.rem(second + d, side)
             picked = matrix[pl.ds(pl.multiple_of(e * block, block), block), :]
             message = lax.dot_general(
@@ -387,45 +405,41 @@
         at = pl.ds(pl.multiple_of(which_core * half_hid + owner * chunk, chunk), chunk)
         return raw.at[at, pl.ds(piece * span, span)]
 
-    sums, more = ring_sum(z, depth, at_z, own_piece, z_term, zs_out, zs_in, zs_send, zs_recv)
-    sent += more
-
-    def to_sibling(which_core, owner, piece, sem):
-        place = raw_view(which_core, owner, piece)
+    def to_sibling(which_core, offset):
+        owner = lax.rem(z + offset, depth)
+        at = pl.ds(pl.multiple_of(which_core * half_hid + owner * chunk, chunk), chunk)
         return pltpu.make_async_remote_copy(
-            src_ref=place,
-            dst_ref=place,
-            send_sem=sg_send.at[sem],
-            recv_sem=sg_recv.at[sem],
+            src_ref=raw.at[at, :],
+            dst_ref=raw.at[at, :],
+            send_sem=sg_send.at[offset],
+            recv_sem=sg_recv.at[offset],
             device_id=sibling,
             device_id_type=MESH,
         )
 
-    expected = []
-
-    def pass_on(owner, piece, sem):
-        going = to_sibling(core, owner, piece, sem)
+    def pass_on(offset):
+        going = to_sibling(core, offset)
         going.start()
         sent.append(going)
-        expected.append((owner, piece, sem))
-
-    for piece in range(PIECES):
+
+    gathered, gather_start, gather_rest = ring_gather(
+        z, depth, at_z, lambda owner, piece: raw_view(core, owner, piece), zg_send, zg_recv, pass_on
+    )
+
+    def summed(piece, value):
         at = pl.ds(pl.multiple_of(core * half_hid + z * chunk, chunk), chunk)
-        raw[at, pl.ds(piece * span, span)] = sums[piece].astype(BF16)
-
-    sent += ring_gather(
-        z,
-        depth,
-        at_z,
-        lambda owner, piece: raw_view(core, owner, piece),
-        zg_send,
-        zg_recv,
-        lambda stream, step, owner, piece: pass_on(owner, piece, PIECES + stream * max(depth // 2, 1) + step),
+        raw[at, pl.ds(piece * span, span)] = value.astype(BF16)
+        gather_start(piece)
+        if piece == PIECES - 1:
+            pass_on(0)
+
+    sent += ring_sum(
+        z, depth, at_z, own_piece, z_term, zs_out, zs_in, zs_send, zs_recv, summed
     )
-    for piece in range(PIECES):
-        pass_on(z, piece, piece)
-    for owner, piece, sem in expected:
-        to_sibling(1 - core, owner, piece, sem).wait_recv()
+    gather_rest()
+    sent += gathered
+    for offset in range(depth):
+        to_sibling(1 - core, offset).wait_recv()
 
     loads[3].wait()
     loads[4].wait()
@@ -472,7 +486,7 @@
     def sum_start(part):
         @pl.loop(0, side)
         def _(i):
-            d = lax.rem(i + side // 2, side)
+            d = turn_of(i)
             f = lax.rem(first + d, side)
             partial = jnp.dot(
                 ret_in[back[part], :],
@@ -489,21 +503,29 @@
                 fs_out[back[part], pl.ds(pl.multiple_of(d * tokens, tokens), tokens)] = partial
                 sum_copy(d, part).start()
 
+    for going in sent:
+        going.wait_send()
     for part in range(2):
         exchange_wait(back[part], part, ret_out, ret_in, ret_send, ret_recv)
         sum_start(part)
+    def result_copy(part):
+        return pltpu.make_async_copy(
+            out_v.at[back[part], :], out_ref.at[back[part], :], out_sem.at[part]
+        )
+
     for part in range(2):
 
         @pl.loop(1, side)
         def _(d):
             sum_copy(d, part).wait()
 
-    total = fs_in[:, pl.ds(0, tokens)].astype(F32)
-    for f in range(1, side):
-        total = total + fs_in[:, pl.ds(f * tokens, tokens)].astype(F32)
-    out_ref[...] = total.astype(BF16)
-    for going in sent:
-        going.wait_send()
+        total = fs_in[back[part], pl.ds(0, tokens)].astype(F32)
+        for f in range(1, side):
+            total = total + fs_in[back[part], pl.ds(f * tokens, tokens)].astype(F32)
+        out_v[back[part], :] = total.astype(BF16)
+        result_copy(part).start()
+    for part in range(2):
+        result_copy(part).wait()
 
 
 def shards(side, depth, out_grad, groups, slots, drops, combine, gate, up, wg, wu, wd):
@@ -522,8 +544,8 @@
         pltpu.VMEM((hidden, places), BF16),
         pltpu.VMEM((feats, hidden), BF16),
         pltpu.VMEM((feats, hidden), BF16),
-        pltpu.VMEM((hidden, feats - feats // 32 * 16), BF16),
-        pltpu.VMEM((hidden, feats // 32 * 16), BF16),
+        pltpu.VMEM((hidden, feats - late_feats(feats)), BF16),
+        pltpu.VMEM((hidden, late_feats(feats)), BF16),
         pltpu.VMEM((feats, hidden), BF16),
         pltpu.VMEM((hidden, places), F32),
         pltpu.VMEM((hidden, places), F32),
@@ -545,6 +567,7 @@
         pltpu.VMEM((feats, places), BF16),
         pltpu.VMEM((feats, width), BF16),
         pltpu.VMEM((feats, width), BF16),
+        pltpu.VMEM((feats, tokens), BF16),
         dma((5,)),
         dma((2, side)),
         dma((2, side)),
@@ -556,19 +579,20 @@
         dma((2 * PIECES, line)),
         dma((2 * PIECES, line)),
         dma((2 * PIECES, line)),
-        dma((PIECES + 2 * PIECES * line,)),
-        dma((PIECES + 2 * PIECES * line,)),
-        dma((2, side)),
-        dma((2, side)),
-        dma((2, side)),
-        dma((2, side)),
+        dma((depth,)),
+        dma((depth,)),
+        dma((2, side)),
+        dma((2, side)),
+        dma((2, side)),
+        dma((2, side)),
+        dma((2,)),
     ]
     vmem, hbm = pl.BlockSpec(memory_space=pltpu.VMEM), pl.BlockSpec(memory_space=pl.ANY)
     columns = pl.pallas_call(
         functools.partial(kernel, side, depth, cap),
         out_shape=jax.ShapeDtypeStruct((feats, tokens), BF16),
         in_specs=[vmem] * 5 + [hbm] * 5,
-        out_specs=vmem,
+        out_specs=hbm,
         scratch_shapes=scratch,
         compiler_params=pltpu.CompilerParams(
             collective_id=0, has_side_effects=True, vmem_limit_bytes=56 * 2**20

time: 118 us -> 112 us (0.949)
  Pallas kernels: 116 us -> 110 us
    pallas_call x1, Pallas kernels: 116 us -> 110 us  [shards(): pl.pallas_call(functools.partial(kernel, side, depth, cap), out_shape=jax...]
where the time goes in v3:
time: 112 us
  Pallas kernels  110 us (98%)
  local copies, waits for them, and re-layouts  1.55 us (1%)
    pallas_call x1, Pallas kernels, shards(): pl.pallas_call(functools.partial(kernel, side, depth, cap), out_shape=jax...  110 us

profile of v3, /device:TPU:1, one launch (start us, length us, event | category | flops | bytes accessed | tf_op | source)
XLA Modules:
  0.0 111.9 jit_solution(4928048925131046931)
XLA Ops:
  0.0 110.3 %shard_map.100 = bf16[448,128]{1,0:T(8,128)(2,1)} custom-call(bf16[448,128]{1,0:T(8,128)(2,1)} %bitcast.19, s32[4,128]{1,0:T(4,128)} %bitcast.20, s32[4,128]{1,0:T(4,128)} %bitcast.21, s32[4,128]{1,0:T(4,128)} %bitcast.22, bf16[4,128]{1,0:T(4,128)(2,1)} %bitcast.23, bf16[1024,1024]{1,0:T(8,128)(2,1)} %bitcast.13, bf16[1024,1024]{1,0:T(8,128)(2,1)} %bitcast.14, ...), custom_call_target="tpu_custom_call" | custom-call | tf_op jit(solution)/shard_map/pallas_call | solution.py:591
  110.3 1.6 %copy.12 = bf16[128,448]{0,1:T(8,128)(2,1)} copy(bf16[128,448]{0,1:T(8,128)(2,1)} %bitcast.18) | data formatting | bytes 229376
